TPU v7x, 32 devices: a whole 2x2x4 slice. The times are simulated.
32 devices in a mesh: grp: 2 (over y), ep: 16 (over z, x, core), sess: 1.
Axes of the slice: x: 2, y: 2, z: 4, core: 2. Of those that a mesh axis runs over, the one named last changes fastest.
Arguments:
- thinker_rows: bfloat16 [1024, 2048], P(('grp', 'ep', 'sess')), parts along dimension 0, may hold values from -6 to 6
- think_route: int32 [1024, 8], P(('grp', 'ep', 'sess')), parts along dimension 0, may hold values from 0 to 15, all different within a row; in each aligned block of 32 rows (0 to 31, 32 to 63, ...) at most 32 rows name the same one
- think_weight: float32 [1024, 8], P(('grp', 'ep', 'sess')), parts along dimension 0, may hold values from 0.1 to 1
- think_gate: bfloat16 [16, 2048, 768], P('ep', None, 'sess'), may hold values from -0.125 to 0.125
- think_up: bfloat16 [16, 2048, 768], P('ep', None, 'sess'), may hold values from -0.125 to 0.125
- think_down: bfloat16 [16, 768, 2048], P('ep', 'sess'), may hold values from -0.21875 to 0.21875
- proj_weight: bfloat16 [2048, 1024], P(None, 'sess'), may hold values from -0.125 to 0.125
- owner_map: int32 [1024], P(('grp', 'ep')), parts along dimension 0, may hold values from 0 to 31, as said below
- talk_gain: float32 [1024], replicated, may hold values from 0.5 to 1.5
- talk_route: int32 [1024, 6], P(('grp', 'ep', 'sess')), parts along dimension 0, may hold values from 0 to 15, all different within a row; in each aligned block of 32 rows (0 to 31, 32 to 63, ...) at most 24 rows name the same one
- talk_weight: float32 [1024, 6], P(('grp', 'ep', 'sess')), parts along dimension 0, may hold values from 0.1 to 1
- talk_gate: bfloat16 [16, 1024, 384], P(('ep', 'sess')), may hold values from -0.1875 to 0.1875
- talk_up: bfloat16 [16, 1024, 384], P(('ep', 'sess')), may hold values from -0.1875 to 0.1875
- talk_down: bfloat16 [16, 384, 1024], P(('ep', 'sess')), may hold values from -0.3125 to 0.3125
Outputs:
- thinker_branch: bfloat16 [1024, 2048], P(('grp', 'ep', 'sess')), parts along dimension 0
- talker_branch: bfloat16 [1024, 1024], P(('grp', 'ep', 'sess')), parts along dimension 0
There are 2 independent parts, one for each index of `grp`. A program takes and returns all parts, laid end to end along the dimension named above; an argument that names none is the same for every part. Nothing has to cross between parts.
Inputs may be any that keep to these rules, and one draw needn't show every extreme that they name: `think_route`: within each aligned block of 32 rows (the rows of one device) no thinker expert is named by more than 32 rows, a bound that some block reaches. `talk_route`: within each aligned block of 32 rows (the rows of one device) no talker expert is named by more than 24 rows, a bound that some block reaches. `owner_map`: each aligned block of 32 entries holds every value of its range exactly once.
All inputs are finite; a program needn't handle non-finite values.
Results may differ from a plain program's by a relative error of at most 0.015.
Values may be sent and summed in bfloat16 or wider, within the bound.
A program may use at most 64 MiB of HBM per device.

v0:
```python
import jax
import jax.numpy as jnp
from jax import lax
from jax.sharding import PartitionSpec as P


def slot_places(route, experts):
    picks = route.shape[0] * route.shape[1]
    chosen = route.reshape(picks)
    onehot = (chosen[:, None] == jnp.arange(experts, dtype=jnp.int32)[None, :]).astype(jnp.int32)
    before = jnp.cumsum(onehot, axis=0) - onehot
    return (chosen, jnp.sum(before * onehot, axis=1))


def pack_rows(row_block, route, experts, capacity):
    chosen, places = slot_places(route, experts)
    target = chosen * capacity + places
    copies = jnp.repeat(row_block, route.shape[1], axis=0)
    buffer = (
        jnp.zeros((experts * capacity, row_block.shape[1]), jnp.bfloat16).at[target].set(copies)
    )
    return (buffer, target)


def combine_rows(returned, target, weights):
    sessions, picks = weights.shape
    gathered = returned[target].astype(jnp.float32).reshape(sessions, picks, returned.shape[1])
    norm_weights = weights / jnp.sum(weights, axis=1, keepdims=True)
    return jnp.sum(gathered * norm_weights[:, :, None], axis=1).astype(jnp.bfloat16)


def swiglu(slab, gate_m, up_m, down_m):
    gate = jnp.dot(slab, gate_m, preferred_element_type=jnp.float32)
    upper = jnp.dot(slab, up_m, preferred_element_type=jnp.float32)
    hidden = (jax.nn.silu(gate) * upper).astype(jnp.bfloat16)
    return jnp.dot(hidden, down_m, preferred_element_type=jnp.float32)


def on_device(
    thinker_rows,
    think_route,
    think_weight,
    think_gate,
    think_up,
    think_down,
    proj_weight,
    owner_map,
    talk_gain,
    talk_route,
    talk_weight,
    talk_gate,
    talk_up,
    talk_down,
):
    sessions = thinker_rows.shape[0]
    features = thinker_rows.shape[1]
    talk_features = talk_gate.shape[1]
    ep_count = lax.axis_size("ep")
    sess_count = lax.axis_size("sess")
    think_picks = think_route.shape[1]
    think_capacity = min(sessions, max(2, 2 * sessions * think_picks // ep_count))
    buffer, target = pack_rows(thinker_rows, think_route, ep_count, think_capacity)
    buffer = buffer.reshape(ep_count, think_capacity, features)
    gate_half = think_gate[0]
    up_half = think_up[0]
    down_half = think_down[0]
    paired = lax.all_gather(buffer, "sess", axis=1, tiled=True)
    arrived = lax.all_to_all(paired, "ep", split_axis=0, concat_axis=0, tiled=True)
    flattened = arrived.reshape(arrived.shape[0] * arrived.shape[1], features)
    result = swiglu(flattened, gate_half, up_half, down_half)
    partial_value = result.reshape(arrived.shape[0], arrived.shape[1], features)
    summed = lax.psum_scatter(partial_value, "sess", scatter_dimension=1, tiled=True).astype(
        jnp.bfloat16
    )
    returned = lax.all_to_all(summed, "ep", split_axis=0, concat_axis=0, tiled=True).reshape(
        ep_count * think_capacity, features
    )
    thinker_branch = combine_rows(returned, target, think_weight)
    projected = jnp.dot(
        lax.all_gather(thinker_branch, "sess", axis=0, tiled=True),
        proj_weight,
        preferred_element_type=jnp.float32,
    ).astype(jnp.bfloat16)
    block_rows = owner_map.shape[0]
    picker = (owner_map[:, None] == jnp.arange(block_rows, dtype=jnp.int32)[None, :]).astype(
        jnp.bfloat16
    )
    selected = jnp.dot(picker, projected, preferred_element_type=jnp.float32).astype(jnp.bfloat16)
    own_rows = lax.all_to_all(selected, "sess", split_axis=0, concat_axis=1, tiled=True).astype(
        jnp.float32
    )
    scale = lax.rsqrt(jnp.mean(own_rows * own_rows, axis=1, keepdims=True) + 1e-06)
    talk_rows = (own_rows * scale * talk_gain[None, :]).astype(jnp.bfloat16)
    talk_experts = ep_count * sess_count
    talk_picks = talk_route.shape[1]
    talk_capacity = min(sessions, max(2, 2 * sessions * talk_picks // talk_experts))
    talk_buffer, talk_target = pack_rows(talk_rows, talk_route, talk_experts, talk_capacity)
    talk_gate_m = talk_gate[0]
    talk_up_m = talk_up[0]
    talk_down_m = talk_down[0]
    sectioned_in = talk_buffer.reshape(talk_experts, talk_capacity, talk_features)
    portion = lax.all_to_all(sectioned_in, ("ep", "sess"), split_axis=0, concat_axis=0, tiled=True)
    flattened = portion.reshape(portion.shape[0] * portion.shape[1], talk_features)
    result = swiglu(flattened, talk_gate_m, talk_up_m, talk_down_m).astype(jnp.bfloat16)
    finished = result.reshape(portion.shape[0], portion.shape[1], talk_features)
    talk_returned = lax.all_to_all(
        finished, ("ep", "sess"), split_axis=0, concat_axis=0, tiled=True
    )
    talk_returned = talk_returned.reshape(talk_experts * talk_capacity, talk_features)
    talker_branch = combine_rows(talk_returned, talk_target, talk_weight)
    return (thinker_branch, talker_branch)


def solution(mesh):
    return jax.shard_map(
        on_device,
        mesh=mesh,
        in_specs=(
            P(("grp", "ep", "sess"), None),
            P(("grp", "ep", "sess"), None),
            P(("grp", "ep", "sess"), None),
            P("ep", None, "sess"),
            P("ep", None, "sess"),
            P("ep", "sess", None),
            P(None, "sess"),
            P(("grp", "ep")),
            P(),
            P(("grp", "ep", "sess"), None),
            P(("grp", "ep", "sess"), None),
            P(("ep", "sess"), None, None),
            P(("ep", "sess"), None, None),
            P(("ep", "sess"), None, None),
        ),
        out_specs=(P(("grp", "ep", "sess"), None), P(("grp", "ep", "sess"), None)),
        check_vma=False,
    )
```

profile of v0, /device:TPU:0, one launch (start us, length us, event | category | flops | bytes accessed | tf_op | source)
XLA Modules:
  0.0 198.9 jit_solution(11233426800232921095)
XLA Ops:
  0.6 0.0 copy-start
  0.6 0.9 copy.19
  1.6 0.1 eq.64
  1.6 0.1 eq.60
  1.7 0.7 broadcast_multiply_fusion.1
  2.4 0.6 reduce-window.14
  3.0 0.2 slice_reduce_fusion.1
  3.2 0.1 copy.18
  3.3 0.1 mul.89
  3.4 0.1 fusion.33
  3.5 4.1 %scatter_custom_fusion = bf16[512,2048]{1,0:T(8,128)(2,1)} fusion(s32[256]{0:T(256)S(1)} %bitcast.89, bf16[]{:T(256)} %constant.11.clone.1, bf16[32,2048]{1,0:T(8,128)(2,1)} %param.14), kind=kCustom, calls=%fused_computation.20 | custom fusion | bytes 2228226 | tf_op jit(solution)/shard_map/scatter | solution.py:20
  7.6 0.0 copy-start.10
  7.6 54.9 %all_to_all.20 = bf16[16,32,2048]{2,1,0:T(8,128)(2,1)S(1)} all-to-all(bf16[16,32,2048]{2,1,0:T(8,128)(2,1)} %bitcast.80), channel_id=1, replica_groups=mesh['grp'=2,'ep'=16,'sess'=1] {'ep'}, dimensions={0} | all-to-all | bytes 4194304 | tf_op jit(solution)/shard_map/all_to_all | solution.py:68
  62.6 0.0 copy-done.10
  62.6 0.0 copy-start.11
  62.6 1.8 fusion.4
  64.4 0.1 copy-done.11
  64.5 1.9 multiply_convert_fusion
  66.4 0.0 copy-done
  66.4 3.1 %fusion.6 = bf16[16,32,2048]{2,1,0:T(8,128)(2,1)} fusion(bf16[16,32,768]{2,1,0:T(8,128)(2,1)S(1)} %bitcast.93, bf16[1,768,2048]{2,1,0:T(8,128)(2,1)S(1)} %copy-done), kind=kOutput, calls=%fused_computation.10 | convolution fusion | flops 1611661312 | bytes 6029312 | tf_op jit(solution)/shard_map/dot_general | solution.py:36
  69.5 0.0 copy-start.4
  69.5 0.0 copy-start.3
  69.5 5.3 %all-to-all-start.1 = ((bf16[16,32,2048]{2,1,0:T(8,128)(2,1)}), bf16[16,32,2048]{2,1,0:T(8,128)(2,1)}, u32[]{:S(2)}, u32[]{:S(2)}) async-start(bf16[16,32,2048]{2,1,0:T(8,128)(2,1)} %fusion.6), calls=%async_computation.1 | async-start | bytes 4194304 | tf_op jit(solution)/shard_map/all_to_all | solution.py:75
  74.8 0.0 copy-done.4
  74.9 0.1 copy.22
  74.9 0.0 copy-done.3
  74.9 0.1 copy.24
  75.0 0.1 eq.68
  75.2 0.6 reduce-window.16
  75.8 0.2 slice_reduce_fusion
  76.0 0.1 copy.23
  76.1 0.1 mul.97
  76.2 0.1 bitcast_bitcast_fusion
  76.3 0.0 copy-start.7
  76.3 39.6 %all-to-all-done.1 = bf16[16,32,2048]{2,1,0:T(8,128)(2,1)} async-done(((bf16[16,32,2048]{2,1,0:T(8,128)(2,1)}), bf16[16,32,2048]{2,1,0:T(8,128)(2,1)}, u32[]{:S(2)}, u32[]{:S(2)}) %all-to-all-start.1) | async-done | bytes 2097184 | tf_op jit(solution)/shard_map/all_to_all | solution.py:75
  116.0 0.0 copy-start.9
  116.0 5.2 %gather_fusion = bf16[256,2048]{1,0:T(8,128)(2,1)} fusion(bf16[512,2048]{1,0:T(8,128)(2,1)} %bitcast.11, s32[1024]{0:T(1024)S(1)} %pad_clamp_fusion.1), kind=kCustom, calls=%fused_computation | custom fusion | bytes 2098176 | tf_op jit(solution)/shard_map/gather | solution.py:27
  121.2 2.2 %fusion.9 = bf16[32,2048]{1,0:T(8,128)(2,1)S(1)} fusion(bf16[256,2048]{1,0:T(8,128)(2,1)} %gather_fusion, f32[32,8]{1,0:T(8,128)S(1)} %copy.22), kind=kLoop, calls=%fused_computation.12 | loop fusion | flops 1507328 | bytes 1180672 | tf_op jit(solution)/shard_map/reduce_sum | solution.py:29
  123.4 0.0 copy-done.9
  123.4 0.0 copy-start.2
  123.4 0.0 copy-start.6
  123.4 3.3 %multiply_reduce_fusion.1 = (f32[32]{0:T(128)S(1)}, f32[32,1024]{1,0:T(8,128)S(1)}) fusion(bf16[32,2048]{1,0:T(8,128)(2,1)S(1)} %fusion.9, bf16[2048,1024]{1,0:T(8,128)(2,1)} %param.20, s32[32]{0:T(128)S(1)} %copy-done.9), kind=kOutput, calls=%fused_computation.38 | convolution fusion | flops 136479712 | bytes 4456704 | tf_op jit(solution)/shard_map/dot_general | solution.py:88
  126.7 0.0 copy-done.2
  126.8 0.0 copy-done.6
  126.8 0.1 multiply_convert_fusion.1
  126.9 0.9 broadcast_in_dim.11
  127.7 1.2 reshape.185
  128.9 0.0 copy-done.7
  128.9 2.3 %scatter_custom_fusion.1 = bf16[384,1024]{1,0:T(8,128)(2,1)} fusion(s32[192]{0:T(256)S(1)} %bitcast.87, bf16[192,1024]{1,0:T(8,128)(2,1)S(1)} %reshape.185, bf16[]{:T(256)} %constant.11.clone.1), kind=kCustom, calls=%fused_computation.34 | custom fusion | bytes 786434 | tf_op jit(solution)/shard_map/scatter | solution.py:20
  131.3 31.5 %all_to_all.21 = bf16[16,24,1024]{2,1,0:T(8,128)(2,1)S(1)} all-to-all(bf16[16,24,1024]{2,1,0:T(8,128)(2,1)} %bitcast.81), channel_id=1, replica_groups=mesh['grp'=2,'ep'=16,'sess'=1] {'ep','sess'}, dimensions={0} | all-to-all | bytes 1572864 | tf_op jit(solution)/shard_map/all_to_all | solution.py:102
  162.8 0.0 copy-start.1
  162.8 0.9 copy-done.1
  163.7 2.5 %fusion.20 = f32[384,384]{1,0:T(8,128)} fusion(bf16[384,1024]{1,0:T(8,128)(2,1)S(1)} %bitcast.82, bf16[1,1024,384]{2,1,0:T(8,128)(2,1)} %param.25), kind=kOutput, calls=%fused_computation.26 | convolution fusion | flops 301989888 | bytes 2162688 | tf_op jit(solution)/shard_map/dot_general | solution.py:33
  166.2 0.0 copy-start.5
  166.2 3.7 %convolution_convert_fusion = bf16[384,1024]{1,0:T(8,128)(2,1)} fusion(bf16[384,1024]{1,0:T(8,128)(2,1)} %bitcast.83, bf16[1,384,1024]{2,1,0:T(8,128)(2,1)} %param.27, bf16[1,1024,384]{2,1,0:T(8,128)(2,1)} %param.26, f32[384,384]{1,0:T(8,128)} %fusion.20), kind=kOutput, calls=%fused_computation.14 | convolution fusion | flops 605257728 | bytes 3735552 | tf_op jit(solution)/shard_map/dot_general | solution.py:36
  169.9 4.3 %all-to-all-start.3 = ((bf16[16,24,1024]{2,1,0:T(8,128)(2,1)}), bf16[16,24,1024]{2,1,0:T(8,128)(2,1)}, u32[]{:S(2)}, u32[]{:S(2)}) async-start(bf16[16,24,1024]{2,1,0:T(8,128)(2,1)} %bitcast.86), calls=%async_computation.3 | async-start | bytes 1572864 | tf_op jit(solution)/shard_map/all_to_all | solution.py:106
  174.2 0.0 copy-done.5
  174.2 0.1 copy.27
  174.3 0.0 copy-done.8
  174.3 0.6 pad_clamp_fusion
  174.9 18.0 %all-to-all-done.3 = bf16[16,24,1024]{2,1,0:T(8,128)(2,1)} async-done(((bf16[16,24,1024]{2,1,0:T(8,128)(2,1)}), bf16[16,24,1024]{2,1,0:T(8,128)(2,1)}, u32[]{:S(2)}, u32[]{:S(2)}) %all-to-all-start.3) | async-done | bytes 786464 | tf_op jit(solution)/shard_map/all_to_all | solution.py:106
  192.9 2.7 %gather_fusion.1 = bf16[192,1024]{1,0:T(8,128)(2,1)S(1)} fusion(bf16[384,1024]{1,0:T(8,128)(2,1)} %bitcast.22, s32[1024]{0:T(1024)} %pad_clamp_fusion), kind=kCustom, calls=%fused_computation.1 | custom fusion | bytes 787200 | tf_op jit(solution)/shard_map/gather | solution.py:27
  195.6 1.1 reshape.156
  196.7 2.3 %multiply_reduce_fusion = bf16[32,1024]{1,0:T(8,128)(2,1)} fusion(f32[32,6,1024]{2,1,0:T(8,128)} %reshape.156, f32[32,6]{1,0:T(8,128)S(1)} %copy.27), kind=kLoop, calls=%fused_computation.22 | loop fusion | flops 360448 | bytes 852736 | tf_op jit(solution)/shard_map/reduce_sum | solution.py:29
  (18 shorter events, 0.2 us)
Async XLA Ops:
  0.6 65.7 %copy-start = (bf16[1,768,2048]{2,1,0:T(8,128)(2,1)S(1)}, bf16[1,768,2048]{2,1,0:T(8,128)(2,1)}, u32[]{:S(2)}) copy-start(bf16[1,768,2048]{2,1,0:T(8,128)(2,1)} %param.19) | copy-start | bytes 9437188
  7.6 54.9 %copy-start.10 = (bf16[1,2048,768]{2,1,0:T(8,128)(2,1)S(1)}, bf16[1,2048,768]{2,1,0:T(8,128)(2,1)}, u32[]{:S(2)}) copy-start(bf16[1,2048,768]{2,1,0:T(8,128)(2,1)} %param.17) | copy-start | bytes 9437188
  62.6 1.9 copy-start.11
  69.5 5.3 %copy-start.4 = (f32[32,8]{0,1:T(8,128)S(1)}, f32[32,8]{0,1:T(8,128)}, u32[]{:S(2)}) copy-start(f32[32,8]{0,1:T(8,128)} %param.16) | copy-start | bytes 3076
  69.5 5.4 %copy-start.3 = (s32[32,6]{0,1:T(8,128)S(1)}, s32[32,6]{0,1:T(8,128)}, u32[]{:S(2)}) copy-start(s32[32,6]{0,1:T(8,128)} %param.23) | copy-start | bytes 2308
  69.5 46.5 %all-to-all-start.1 = ((bf16[16,32,2048]{2,1,0:T(8,128)(2,1)}), bf16[16,32,2048]{2,1,0:T(8,128)(2,1)}, u32[]{:S(2)}, u32[]{:S(2)}) async-start(bf16[16,32,2048]{2,1,0:T(8,128)(2,1)} %fusion.6), calls=%async_computation.1 | async-start | bytes 4194304 | tf_op jit(solution)/shard_map/all_to_all | solution.py:75
  76.3 52.6 %copy-start.7 = (s32[192,1]{0,1:T(1,128)}, s32[192,1]{0,1:T(1,128)S(1)}, u32[]{:S(2)}) copy-start(s32[192,1]{0,1:T(1,128)S(1)} %compare_select_fusion) | copy-start | bytes 2308
  116.0 7.4 %copy-start.9 = (s32[32]{0:T(128)S(1)}, s32[32]{0:T(128)}, u32[]{:S(2)}) copy-start(s32[32]{0:T(128)} %param.21) | copy-start | bytes 388
  123.4 3.3 %copy-start.2 = (bf16[32,2048]{1,0:T(8,128)(2,1)}, bf16[32,2048]{1,0:T(8,128)(2,1)S(1)}, u32[]{:S(2)}) copy-start(bf16[32,2048]{1,0:T(8,128)(2,1)S(1)} %fusion.9) | copy-start | bytes 393220
  123.4 3.3 %copy-start.6 = (f32[1024]{0:T(1024)S(1)}, f32[1024]{0:T(1024)}, u32[]{:S(2)}) copy-start(f32[1024]{0:T(1024)} %param.22) | copy-start | bytes 12292
  162.8 0.9 copy-start.1
  166.2 8.0 %copy-start.5 = (f32[32,6]{0,1:T(8,128)S(1)}, f32[32,6]{0,1:T(8,128)}, u32[]{:S(2)}) copy-start(f32[32,6]{0,1:T(8,128)} %param.24) | copy-start | bytes 2308
  166.2 8.1 %copy-start.8 = (s32[192,1]{0,1:T(1,128)S(1)}, s32[192,1]{0,1:T(1,128)}, u32[]{:S(2)}) copy-start(s32[192,1]{0,1:T(1,128)} %copy-done.7) | copy-start | bytes 2308
  169.9 23.0 %all-to-all-start.3 = ((bf16[16,24,1024]{2,1,0:T(8,128)(2,1)}), bf16[16,24,1024]{2,1,0:T(8,128)(2,1)}, u32[]{:S(2)}, u32[]{:S(2)}) async-start(bf16[16,24,1024]{2,1,0:T(8,128)(2,1)} %bitcast.86), calls=%async_computation.3 | async-start | bytes 1572864 | tf_op jit(solution)/shard_map/all_to_all | solution.py:106
where the time goes:
time: 200 us; the launch traced here: 199 us
  blocking collectives  86.4 us (43%)
  waiting for transfers between devices  57.6 us (29%)
  local copies, waits for them, and re-layouts  20.7 us (10%)
  matrix products  16.4 us (8%)
  starting transfers between devices  9.58 us (5%)
  other arithmetic  7.37 us (4%)
    all_to_all x1, blocking collectives, on_device(): lax.all_to_all(paired, 'ep', split_axis=0, concat_axis=0, tiled=True)  54.9 us
    all_to_all x1, waiting for transfers between devices, on_device(): lax.all_to_all(summed, 'ep', split_axis=0, concat_axis=0, tiled=True)  39.6 us
    all_to_all x1, blocking collectives, on_device(): lax.all_to_all(sectioned_in, ('ep', 'sess'), split_axis=0, concat_axis=0,...  31.5 us
    all_to_all x1, waiting for transfers between devices, on_device(): lax.all_to_all(finished, ('ep', 'sess'), split_axis=0, concat_axis=0, til...  18 us
    gather x2, local copies, waits for them, and re-layouts, combine_rows(): returned[target].astype(jnp.float32)  7.89 us
    dot_general x2, matrix products, swiglu(): return jnp.dot(hidden, down_m, preferred_element_type=jnp.float32)  6.85 us
    scatter x2, local copies, waits for them, and re-layouts, pack_rows(): jnp.zeros((experts * capacity, row_block.shape[1]), jnp.bfloat16).at[target]  6.46 us
    all_to_all x1, starting transfers between devices, on_device(): lax.all_to_all(summed, 'ep', split_axis=0, concat_axis=0, tiled=True)  5.3 us
  transfers between devices with their start and end apart: 2, of which 2 were waited for; matrix products, arithmetic and copies ran while one was open for 1% of the time, Pallas kernels for 0%

commit v1 on v0

--- a/solution.py
+++ b/solution.py
@@ -1,19 +1,28 @@
+import functools
+
 import jax
 import jax.numpy as jnp
 from jax import lax
+from jax.experimental import pallas as pl
+from jax.experimental.pallas import tpu as pltpu
 from jax.sharding import PartitionSpec as P
 
-
-def slot_places(route, experts):
+LANES = 128
+TILE = 256
+F32 = jnp.float32
+BF16 = jnp.bfloat16
+
+
+def slot_places(route):
     picks = route.shape[0] * route.shape[1]
     chosen = route.reshape(picks)
-    onehot = (chosen[:, None] == jnp.arange(experts, dtype=jnp.int32)[None, :]).astype(jnp.int32)
-    before = jnp.cumsum(onehot, axis=0) - onehot
-    return (chosen, jnp.sum(before * onehot, axis=1))
+    order = jnp.arange(picks, dtype=jnp.int32)
+    earlier = (chosen[:, None] == chosen[None, :]) & (order[None, :] < order[:, None])
+    return (chosen, jnp.sum(earlier.astype(jnp.int32), axis=1))
 
 
 def pack_rows(row_block, route, experts, capacity):
-    chosen, places = slot_places(route, experts)
+    chosen, places = slot_places(route)
     target = chosen * capacity + places
     copies = jnp.repeat(row_block, route.shape[1], axis=0)
     buffer = (
@@ -36,7 +45,7 @@
     return jnp.dot(hidden, down_m, preferred_element_type=jnp.float32)
 
 
-def on_device(
+def packed_on_device(
     thinker_rows,
     think_route,
     think_weight,
@@ -111,6 +120,405 @@
     return (thinker_branch, talker_branch)
 
 
+def dense_weights(route, weights, experts):
+    rows, picks = route.shape
+    lane = lax.broadcasted_iota(jnp.int32, (rows, LANES), 1)
+    norm = weights / jnp.sum(weights, axis=1, keepdims=True)
+    parts = jnp.zeros((rows, LANES), F32)
+    for k in range(picks):
+        value = norm[:, k : k + 1]
+        high = value.astype(BF16).astype(F32)
+        middle = (value - high).astype(BF16).astype(F32)
+        low = value - high - middle
+        chosen = route[:, k : k + 1]
+        parts = parts + jnp.where(lane == chosen, high, 0.0)
+        parts = parts + jnp.where(lane == chosen + experts, middle, 0.0)
+        parts = parts + jnp.where(lane == chosen + 2 * experts, low, 0.0)
+    return parts.astype(BF16)
+
+
+class Place:
+    def __init__(self, layers):
+        self.layers = layers
+        self.ep = lax.axis_index("ep")
+        self.z = self.ep // 4
+        self.x = (self.ep // 2) % 2
+        self.c = self.ep % 2
+        self.sibling = {"ep": self.ep + 1 - 2 * self.c}
+        self.across = {"ep": self.ep + 2 - 4 * self.x}
+        self.up = {"ep": self.ep + 4}
+        self.down = {"ep": self.ep - 4}
+        self.has_up = self.z < layers - 1
+        self.has_down = self.z > 0
+
+
+def remote(src, dst, send_sem, recv_sem, peer):
+    return pltpu.make_async_remote_copy(
+        src_ref=src,
+        dst_ref=dst,
+        send_sem=send_sem,
+        recv_sem=recv_sem,
+        device_id=peer,
+        device_id_type=pl.DeviceIdType.MESH,
+    )
+
+
+def greet(place):
+    barrier = pltpu.get_barrier_semaphore()
+
+    def signal(peer):
+        pl.semaphore_signal(barrier, inc=1, device_id=peer, device_id_type=pl.DeviceIdType.MESH)
+
+    signal(place.sibling)
+    signal(place.across)
+
+    @pl.when(place.has_up)
+    def _():
+        signal(place.up)
+
+    @pl.when(place.has_down)
+    def _():
+        signal(place.down)
+
+    count = 2 + jnp.where(place.has_up, 1, 0) + jnp.where(place.has_down, 1, 0)
+    pl.semaphore_wait(barrier, count)
+
+
+def mixture_phase(place, features, gate_w, up_w, down_w, wait_weights, scratch):
+    (held, hidden, scaled, partial, core_in, x_out, x_in, z_out, z_in,
+     zs, zr, xs, xr, cs, cr, rs_cs, rs_cr, rs_xs, rs_xr, rs_zs, rs_zr) = scratch
+    z, x, c, layers = place.z, place.x, place.c, place.layers
+    rows = held.shape[3]
+    group = 2 * layers * rows
+    ff = gate_w.shape[1]
+
+    def z_copy(way, step, block):
+        slot = held.at[x, c, block]
+        return remote(slot, slot, zs.at[way, step], zr.at[way, step], (place.up, place.down)[way])
+
+    def x_copy(side, block):
+        slot = held.at[side, c, block]
+        return remote(slot, slot, xs.at[block], xr.at[block], place.across)
+
+    def c_copy(side, core, block):
+        slot = held.at[side, core, block]
+        return remote(slot, slot, cs.at[side, block], cr.at[side, block], place.sibling)
+
+    def fan(block):
+        x_copy(x, block).start()
+        c_copy(x, c, block).start()
+
+    def arrivals(step, then):
+        @pl.when(z - 1 - step >= 0)
+        def _():
+            then(0, z - 1 - step)
+
+        @pl.when(z + 1 + step < layers)
+        def _():
+            then(1, z + 1 + step)
+
+    def from_across(block):
+        x_copy(1 - x, block).wait_recv()
+        c_copy(1 - x, c, block).start()
+
+    ahead = (place.has_up, place.has_down)
+    for way in range(2):
+        @pl.when(ahead[way])
+        def _(way=way):
+            z_copy(way, 0, z).start()
+
+    fan(z)
+    for step in range(layers - 1):
+        def pass_on(way, block, step=step):
+            z_copy(way, step, block).wait_recv()
+
+            @pl.when(ahead[way])
+            def _():
+                z_copy(way, step + 1, block).start()
+
+            fan(block)
+
+        arrivals(step, pass_on)
+        if step == 0:
+            from_across(z)
+        else:
+            arrivals(step - 1, lambda way, block: from_across(block))
+
+    def from_sibling(side):
+        for block in range(layers):
+            c_copy(side, 1 - c, block).wait_recv()
+
+    def enter(side, which):
+        def tile(i, carry):
+            at = pl.ds(pl.multiple_of(i * width, width), width)
+            slab = held[side, :, :, :, :features].reshape(group, features)
+            gate = jnp.dot(slab, gate_w[:, at], preferred_element_type=F32)
+            upper = jnp.dot(slab, up_w[:, at], preferred_element_type=F32)
+            hidden[which, :, at] = (gate * (1.0 / (1.0 + jnp.exp(-gate))) * upper).astype(BF16)
+            return carry
+
+        width = TILE if ff % TILE == 0 else LANES
+        lax.fori_loop(0, ff // width, tile, 0)
+        parts = held[side, :, :, :, features:].reshape(group, LANES).astype(F32)
+        lane = lax.broadcasted_iota(jnp.int32, (group, LANES), 1)
+        experts = 4 * layers
+        mine = (lane % experts == place.ep) & (lane < 3 * experts)
+        scaled[which] = jnp.sum(jnp.where(mine, parts, 0.0), axis=1, keepdims=True)
+
+    def leave(side, which):
+        def tile(i, carry):
+            at = pl.ds(pl.multiple_of(i * TILE, TILE), TILE)
+            out = jnp.dot(hidden[which], down_w[:, at], preferred_element_type=F32)
+            out = (out * scaled[which]).astype(BF16)
+            partial[side, :, :, :, at] = out.reshape(2, layers, rows, TILE)
+            return carry
+
+        lax.fori_loop(0, features // TILE, tile, 0)
+
+    from_sibling(x)
+    wait_weights(0)
+    enter(x, 0)
+    arrivals(layers - 2, lambda way, block: from_across(block))
+    from_sibling(1 - x)
+    enter(1 - x, 1)
+    wait_weights(1)
+    leave(1 - x, 1)
+
+    def core_sum(side, which):
+        return remote(
+            partial.at[side, 1 - c], core_in.at[which], rs_cs.at[which], rs_cr.at[which],
+            place.sibling,
+        )
+
+    def x_sum(block):
+        return remote(
+            x_out.at[block], x_in.at[block], rs_xs.at[block], rs_xr.at[block], place.across
+        )
+
+    def z_sum(way, block):
+        return remote(
+            z_out.at[block], z_in.at[way, block], rs_zs.at[block], rs_zr.at[way, block],
+            (place.up, place.down)[way],
+        )
+
+    def outward(then):
+        for far in range(layers - 1, 0, -1):
+            @pl.when(z + far < layers)
+            def _(far=far):
+                then(0, z + far)
+
+            @pl.when(z - far >= 0)
+            def _(far=far):
+                then(1, z - far)
+
+    core_sum(1 - x, 1).start()
+    leave(x, 0)
+    core_sum(x, 0).start()
+    core_sum(1 - x, 1).wait_recv()
+
+    def send_across(way, block):
+        total = partial[1 - x, c, block].astype(F32) + core_in[1, block].astype(F32)
+        x_out[block] = total.astype(BF16)
+        x_sum(block).start()
+
+    outward(send_across)
+    send_across(0, z)
+    core_sum(x, 0).wait_recv()
+
+    def chip_total(block):
+        total = partial[x, c, block].astype(F32) + core_in[0, block].astype(F32)
+        x_sum(block).wait_recv()
+        return total + x_in[block].astype(F32)
+
+    behind = (place.has_down, place.has_up)
+
+    def send_along(way, block):
+        total = chip_total(block)
+
+        @pl.when(behind[way])
+        def _():
+            z_sum(way, block).wait_recv()
+
+        z_out[block] = (total + z_in[way, block].astype(F32)).astype(BF16)
+        z_sum(way, block).start()
+
+    outward(send_along)
+    total = chip_total(z)
+    for way in range(2):
+        @pl.when(behind[way])
+        def _(way=way):
+            z_sum(way, z).wait_recv()
+
+        total = total + z_in[way, z].astype(F32)
+
+    def finish():
+        for way in range(2):
+            @pl.when(ahead[way])
+            def _(way=way):
+                z_copy(way, 0, z).wait_send()
+
+        for step in range(layers - 1):
+            def sent(way, block, step=step):
+                @pl.when(ahead[way])
+                def _():
+                    z_copy(way, step + 1, block).wait_send()
+
+            arrivals(step, sent)
+        for block in range(layers):
+            x_copy(x, block).wait_send()
+            c_copy(x, c, block).wait_send()
+            c_copy(1 - x, c, block).wait_send()
+            x_sum(block).wait_send()
+        core_sum(x, 0).wait_send()
+        core_sum(1 - x, 1).wait_send()
+        outward(lambda way, block: z_sum(way, block).wait_send())
+
+    return total, finish
+
+
+def clear_ends(place, z_in):
+    for way, has in enumerate((place.has_down, place.has_up)):
+        @pl.when(jnp.logical_not(has))
+        def _(way=way):
+            z_in[way] = jnp.zeros(z_in.shape[1:], z_in.dtype)
+
+
+PHASE_REFS = 21
+
+
+def step_kernel(
+    layers,
+    rows_ref, route_ref, weight_ref, gain_ref, owner_ref, talk_route_ref, talk_weight_ref,
+    gate_hbm, up_hbm, down_hbm, proj_hbm, tgate_hbm, tup_hbm, tdown_hbm,
+    think_out, talk_out,
+    gate_v, up_v, down_v, proj_v, tgate_v, tup_v, tdown_v, load_sem,
+    *phases,
+):
+    place = Place(layers)
+    think, talk = phases[:PHASE_REFS], phases[PHASE_REFS:]
+    pairs = (
+        (gate_hbm.at[0], gate_v), (up_hbm.at[0], up_v), (down_hbm.at[0], down_v),
+        (proj_hbm, proj_v),
+        (tgate_hbm.at[0], tgate_v), (tup_hbm.at[0], tup_v), (tdown_hbm.at[0], tdown_v),
+    )
+    loads = [
+        pltpu.make_async_copy(src, dst, load_sem.at[i]) for i, (src, dst) in enumerate(pairs)
+    ]
+    for load in loads:
+        load.start()
+    experts = 4 * layers
+    features = rows_ref.shape[1]
+    talk_features = gain_ref.shape[1]
+    z, x, c = place.z, place.x, place.c
+    held, talk_held = think[0], talk[0]
+    held[x, c, z, :, :features] = rows_ref[...]
+    held[x, c, z, :, features:] = dense_weights(route_ref[...], weight_ref[...], experts)
+    talk_held[x, c, z, :, talk_features:] = dense_weights(
+        talk_route_ref[...], talk_weight_ref[...], experts
+    )
+    clear_ends(place, think[8])
+    clear_ends(place, talk[8])
+    greet(place)
+
+    def wait_think(stage):
+        for load in (loads[:2], loads[2:3])[stage]:
+            load.wait()
+
+    def wait_talk(stage):
+        for load in (loads[4:6], loads[6:7])[stage]:
+            load.wait()
+
+    total, finish_think = mixture_phase(place, features, gate_v, up_v, down_v, wait_think, think)
+    branch = total.astype(BF16)
+    think_out[...] = branch
+    loads[3].wait()
+    projected = jnp.dot(branch, proj_v[...], preferred_element_type=F32).astype(BF16)
+    count = owner_ref.shape[0]
+    spot = lax.broadcasted_iota(jnp.int32, (count, count), 1)
+    picker = jnp.where(owner_ref[...] == spot, 1.0, 0.0).astype(BF16)
+    own_rows = jnp.dot(picker, projected, preferred_element_type=F32)
+    scale = lax.rsqrt(jnp.mean(own_rows * own_rows, axis=1, keepdims=True) + 1e-06)
+    talk_held[x, c, z, :, :talk_features] = (own_rows * scale * gain_ref[...]).astype(BF16)
+    total, finish_talk = mixture_phase(
+        place, talk_features, tgate_v, tup_v, tdown_v, wait_talk, talk
+    )
+    talk_out[...] = total.astype(BF16)
+    finish_think()
+    finish_talk()
+
+
+def phase_scratch(layers, rows, features, ff):
+    group = 2 * layers * rows
+    dma = pltpu.SemaphoreType.DMA
+    block = (layers, rows, features)
+    return [
+        pltpu.VMEM((2, 2, layers, rows, features + LANES), BF16),
+        pltpu.VMEM((2, group, ff), BF16),
+        pltpu.VMEM((2, group, 1), F32),
+        pltpu.VMEM((2, 2) + block, BF16),
+        pltpu.VMEM((2,) + block, BF16),
+        pltpu.VMEM(block, BF16),
+        pltpu.VMEM(block, BF16),
+        pltpu.VMEM(block, BF16),
+        pltpu.VMEM((2,) + block, BF16),
+        dma((2, layers)), dma((2, layers)),
+        dma((layers,)), dma((layers,)),
+        dma((2, layers)), dma((2, layers)),
+        dma((2,)), dma((2,)),
+        dma((layers,)), dma((layers,)),
+        dma((layers,)), dma((2, layers)),
+    ]
+
+
+def dense_on_device(
+    thinker_rows, think_route, think_weight, think_gate, think_up, think_down, proj_weight,
+    owner_map, talk_gain, talk_route, talk_weight, talk_gate, talk_up, talk_down,
+):
+    layers = lax.axis_size("ep") // 4
+    rows, features = thinker_rows.shape
+    talk_features, talk_ff = talk_gate.shape[1:]
+    ff = think_gate.shape[2]
+    vmem = pl.BlockSpec(memory_space=pltpu.VMEM)
+    hbm = pl.BlockSpec(memory_space=pl.ANY)
+    weights = (think_gate, think_up, think_down, proj_weight, talk_gate, talk_up, talk_down)
+    sizes = [w.shape[-2:] for w in weights]
+    all_rows = 4 * layers * rows
+    return pl.pallas_call(
+        functools.partial(step_kernel, layers),
+        out_shape=(
+            jax.ShapeDtypeStruct((rows, features), BF16),
+            jax.ShapeDtypeStruct((rows, talk_features), BF16),
+        ),
+        in_specs=[vmem] * 7 + [hbm] * 7,
+        out_specs=(vmem, vmem),
+        scratch_shapes=[pltpu.VMEM(size, BF16) for size in sizes]
+        + [pltpu.SemaphoreType.DMA((len(sizes),))]
+        + phase_scratch(layers, rows, features, ff)
+        + phase_scratch(layers, rows, talk_features, talk_ff),
+        compiler_params=pltpu.CompilerParams(
+            collective_id=0, has_side_effects=True, vmem_limit_bytes=56 * 1024 * 1024
+        ),
+        cost_estimate=pl.CostEstimate(
+            flops=6 * all_rows * (features * ff + talk_features * talk_ff),
+            bytes_accessed=2 * sum(a * b for a, b in sizes),
+            transcendentals=all_rows * (ff + talk_ff),
+        ),
+    )(
+        thinker_rows, think_route, think_weight, talk_gain[None, :], owner_map[:, None],
+        talk_route, talk_weight, *weights,
+    )
+
+
+def on_device(*arguments):
+    rows, picks = arguments[1].shape
+    talk_rows, talk_picks = arguments[9].shape
+    ep_count = lax.axis_size("ep")
+    whole = lax.axis_size("sess") == 1 and ep_count % 4 == 0 and 3 * ep_count <= LANES
+    if whole and ep_count >= 8 and 2 * picks >= ep_count and arguments[0].shape[1] % TILE == 0:
+        return dense_on_device(*arguments)
+    return packed_on_device(*arguments)
+
+
 def solution(mesh):
     return jax.shard_map(
         on_device,

time: 200 us -> 94.4 us (0.47)
  blocking collectives: 86.4 us -> 0 us
  Pallas kernels: 0 us -> 83.6 us
  waiting for transfers between devices: 57.6 us -> 0 us
  matrix products: 16.4 us -> 0 us
  local copies, waits for them, and re-layouts: 20.7 us -> 9.84 us
  starting transfers between devices: 9.58 us -> 0 us
  other arithmetic: 7.37 us -> 0 us
    all_to_all x2 -> x0, blocking collectives: 86.4 us -> none  [the longest x1 54.9 us: on_device(): lax.all_to_all(paired, 'ep', split_axis=0, concat_axis=0, tiled=True)]
    pallas_call x0 -> x1, Pallas kernels: none -> 83.6 us  [dense_on_device(): pl.pallas_call(functools.partial(step_kernel, layers), out_shape=(jax.Sha...]
    all_to_all x2 -> x0, waiting for transfers between devices: 57.6 us -> none  [the longest x1 39.6 us: on_device(): lax.all_to_all(summed, 'ep', split_axis=0, concat_axis=0, tiled=True)]
    dot_general x6 -> x0, matrix products: 16.4 us -> none  [the longest x2 6.85 us: swiglu(): return jnp.dot(hidden, down_m, preferred_element_type=jnp.float32)]
    all_to_all x2 -> x0, starting transfers between devices: 9.58 us -> none  [the longest x1 5.3 us: on_device(): lax.all_to_all(summed, 'ep', split_axis=0, concat_axis=0, tiled=True)]
    gather x2 -> x0, local copies, waits for them, and re-layouts: 7.89 us -> none  [combine_rows(): returned[target].astype(jnp.float32)]
    unnamed x26 -> x6, local copies, waits for them, and re-layouts: 2.03 us -> 8.51 us
    scatter x2 -> x0, local copies, waits for them, and re-layouts: 6.46 us -> none  [pack_rows(): jnp.zeros((experts * capacity, row_block.shape[1]), jnp.bfloat16).at[target]]
  transfers between devices with their start and end apart: 2 -> 0, of which waited for: 2 -> 0; matrix products, arithmetic and copies ran while one was open for 1% -> 0% of each run, Pallas kernels for 0% -> 0%
where the time goes in v1:
time: 94.4 us; the launch traced here: 94.1 us
  Pallas kernels  83.6 us (89%)
  local copies, waits for them, and re-layouts  9.84 us (10%)
    pallas_call x1, Pallas kernels, dense_on_device(): pl.pallas_call(functools.partial(step_kernel, layers), out_shape=(jax.Sha...  83.6 us
    unnamed x6, local copies, waits for them, and re-layouts  8.51 us

profile of v1, /device:TPU:0, one launch (start us, length us, event | category | flops | bytes accessed | tf_op | source)
XLA Modules:
  0.0 94.1 jit_solution(15875511399110316649)
XLA Ops:
  0.6 1.4 %copy.16.route_ref = s32[32,8]{1,0:T(8,128)} copy(s32[32,8]{0,1:T(8,128)} %param.15) | data formatting | bytes 2048 | tf_op args[1]
  2.0 1.4 %copy.17.weight_ref = f32[32,8]{1,0:T(8,128)} copy(f32[32,8]{0,1:T(8,128)} %param.16) | data formatting | bytes 2048 | tf_op args[2]
  3.4 1.3 %copy.18.owner_ref = s32[32,1]{1,0:T(8,128)} copy(s32[32,1]{0,1:T(1,128)} %bitcast.2) | data formatting | bytes 256 | tf_op jit(solution)/shard_map/broadcast_in_dim | solution.py:507
  4.7 1.4 %copy.19.talk_route_ref = s32[32,6]{1,0:T(8,128)} copy(s32[32,6]{0,1:T(8,128)} %param.23) | data formatting | bytes 1536 | tf_op args[9]
  6.1 1.4 %copy.20.talk_weight_ref = f32[32,6]{1,0:T(8,128)} copy(f32[32,6]{0,1:T(8,128)} %param.24) | data formatting | bytes 1536 | tf_op args[10]
  7.4 83.6 %shard_map.149 = (bf16[32,2048]{1,0:T(8,128)(2,1)}, bf16[32,1024]{1,0:T(8,128)(2,1)}) custom-call(bf16[32,2048]{1,0:T(8,128)(2,1)} %rows_ref.1, s32[32,8]{1,0:T(8,128)} %copy.16.route_ref, f32[32,8]{1,0:T(8,128)} %copy.17.weight_ref, f32[1,1024]{1,0:T(1,128)} %bitcast.3, s32[32,1]{1,0:T(8,128)} %copy.18.owner_ref, s32[32,6]{1,0:T(8,128)} %copy.19.talk_route_ref, ...), custom_call_target="tpu_custom_call" | custom-call | flops 6039797760 | bytes 15990784 | tf_op jit(solution)/shard_map/pallas_call | solution.py:486
  91.0 1.6 %copy.23 = bf16[32,2048]{1,0:T(8,128)(2,1)} copy(bf16[32,2048]{1,0:T(8,128)(2,1)} %get-tuple-element.4) | data formatting | bytes 262144
  92.6 1.5 %copy.24 = bf16[32,1024]{1,0:T(8,128)(2,1)} copy(bf16[32,1024]{1,0:T(8,128)(2,1)} %get-tuple-element.5) | data formatting | bytes 131072

commit v2 on v0

--- a/solution.py
+++ b/solution.py
@@ -1,19 +1,28 @@
+import functools
+
 import jax
 import jax.numpy as jnp
 from jax import lax
+from jax.experimental import pallas as pl
+from jax.experimental.pallas import tpu as pltpu
 from jax.sharding import PartitionSpec as P
 
-
-def slot_places(route, experts):
+LANES = 128
+TILE = 256
+F32 = jnp.float32
+BF16 = jnp.bfloat16
+
+
+def slot_places(route):
     picks = route.shape[0] * route.shape[1]
     chosen = route.reshape(picks)
-    onehot = (chosen[:, None] == jnp.arange(experts, dtype=jnp.int32)[None, :]).astype(jnp.int32)
-    before = jnp.cumsum(onehot, axis=0) - onehot
-    return (chosen, jnp.sum(before * onehot, axis=1))
+    order = jnp.arange(picks, dtype=jnp.int32)
+    earlier = (chosen[:, None] == chosen[None, :]) & (order[None, :] < order[:, None])
+    return (chosen, jnp.sum(earlier.astype(jnp.int32), axis=1))
 
 
 def pack_rows(row_block, route, experts, capacity):
-    chosen, places = slot_places(route, experts)
+    chosen, places = slot_places(route)
     target = chosen * capacity + places
     copies = jnp.repeat(row_block, route.shape[1], axis=0)
     buffer = (
@@ -36,7 +45,7 @@
     return jnp.dot(hidden, down_m, preferred_element_type=jnp.float32)
 
 
-def on_device(
+def packed_on_device(
     thinker_rows,
     think_route,
     think_weight,
@@ -111,6 +120,498 @@
     return (thinker_branch, talker_branch)
 
 
+def dense_weights(route, weights, experts):
+    picks, rows = route.shape
+    spot = lax.broadcasted_iota(jnp.int32, (LANES, rows), 0)
+    norm = weights / jnp.sum(weights, axis=0, keepdims=True)
+    parts = jnp.zeros((LANES, rows), F32)
+    for k in range(picks):
+        value = norm[k : k + 1]
+        high = value.astype(BF16).astype(F32)
+        middle = (value - high).astype(BF16).astype(F32)
+        low = value - high - middle
+        chosen = route[k : k + 1]
+        parts = parts + jnp.where(spot == chosen, high, 0.0)
+        parts = parts + jnp.where(spot == chosen + experts, middle, 0.0)
+        parts = parts + jnp.where(spot == chosen + 2 * experts, low, 0.0)
+    down = lax.broadcasted_iota(jnp.int32, (rows, rows), 0)
+    along = lax.broadcasted_iota(jnp.int32, (rows, rows), 1)
+    turned = lax.dot_general(
+        jnp.where(down == along, 1.0, 0.0).astype(BF16), parts.astype(BF16),
+        (((1,), (1,)), ((), ())), preferred_element_type=F32,
+    )
+    return turned.astype(BF16)
+
+
+class Place:
+    def __init__(self, layers):
+        self.layers = layers
+        self.ep = lax.axis_index("ep")
+        self.z = self.ep // 4
+        self.x = (self.ep // 2) % 2
+        self.c = self.ep % 2
+        self.sibling = {"ep": self.ep + 1 - 2 * self.c}
+        self.across = {"ep": self.ep + 2 - 4 * self.x}
+        self.up = {"ep": self.ep + 4}
+        self.down = {"ep": self.ep - 4}
+        self.has_up = self.z < layers - 1
+        self.has_down = self.z > 0
+
+
+def remote(src, dst, send_sem, recv_sem, peer):
+    return pltpu.make_async_remote_copy(
+        src_ref=src,
+        dst_ref=dst,
+        send_sem=send_sem,
+        recv_sem=recv_sem,
+        device_id=peer,
+        device_id_type=pl.DeviceIdType.MESH,
+    )
+
+
+def greet(place):
+    barrier = pltpu.get_barrier_semaphore()
+
+    def signal(peer):
+        pl.semaphore_signal(barrier, inc=1, device_id=peer, device_id_type=pl.DeviceIdType.MESH)
+
+    signal(place.sibling)
+    signal(place.across)
+
+    @pl.when(place.has_up)
+    def _():
+        signal(place.up)
+
+    @pl.when(place.has_down)
+    def _():
+        signal(place.down)
+
+    count = 2 + jnp.where(place.has_up, 1, 0) + jnp.where(place.has_down, 1, 0)
+    pl.semaphore_wait(barrier, count)
+
+
+class Mixture:
+    def __init__(self, place, features, weights, scratch):
+        self.place, self.features, self.weights = place, features, weights
+        (self.held, self.hidden, self.scaled, self.partial, self.core_in, self.x_out,
+         self.x_in, self.z_out, self.z_in,
+         self.zs, self.zr, self.xs, self.xr, self.cs, self.cr,
+         self.rs_cs, self.rs_cr, self.rs_xs, self.rs_xr, self.rs_zs, self.rs_zr) = scratch
+        self.layers = place.layers
+        self.ahead = (place.has_up, place.has_down)
+        self.behind = (place.has_down, place.has_up)
+        self.peers = (place.up, place.down)
+
+    def z_copy(self, way, step, block):
+        slot = self.held.at[self.place.x, self.place.c, block]
+        return remote(slot, slot, self.zs.at[way, step], self.zr.at[way, step], self.peers[way])
+
+    def x_copy(self, side, block):
+        slot = self.held.at[side, self.place.c, block]
+        return remote(slot, slot, self.xs.at[block], self.xr.at[block], self.place.across)
+
+    def c_copy(self, side, core, block):
+        slot = self.held.at[side, core, block]
+        return remote(
+            slot, slot, self.cs.at[side, block], self.cr.at[side, block], self.place.sibling
+        )
+
+    def fan(self, block):
+        self.x_copy(self.place.x, block).start()
+        self.c_copy(self.place.x, self.place.c, block).start()
+
+    def arrivals(self, step, then):
+        z = self.place.z
+
+        @pl.when(z - 1 - step >= 0)
+        def _():
+            then(0, z - 1 - step)
+
+        @pl.when(z + 1 + step < self.layers)
+        def _():
+            then(1, z + 1 + step)
+
+    def from_across(self, block):
+        side = 1 - self.place.x
+        self.x_copy(side, block).wait_recv()
+        self.c_copy(side, self.place.c, block).start()
+
+    def gather_start(self):
+        z = self.place.z
+        for way in range(2):
+            @pl.when(self.ahead[way])
+            def _(way=way):
+                self.z_copy(way, 0, z).start()
+
+        self.fan(z)
+
+    def gather_step(self, step):
+        def pass_on(way, block):
+            self.z_copy(way, step, block).wait_recv()
+
+            @pl.when(self.ahead[way])
+            def _():
+                self.z_copy(way, step + 1, block).start()
+
+            self.fan(block)
+
+        if step < self.layers - 1:
+            self.arrivals(step, pass_on)
+        if step == 0:
+            self.from_across(self.place.z)
+        else:
+            self.arrivals(step - 1, lambda way, block: self.from_across(block))
+
+    def gather_end(self):
+        for side in range(2):
+            for block in range(self.layers):
+                self.c_copy(side, 1 - self.place.c, block).wait_recv()
+
+    def enter(self, first, last):
+        gate_w, up_w, _ = self.weights
+        group = self.hidden.shape[0]
+        ff = gate_w.shape[1]
+        width = TILE if ff % TILE == 0 else LANES
+
+        def tile(i, carry):
+            at = pl.ds(pl.multiple_of(i * width, width), width)
+            slab = self.held[:, :, :, :, : self.features].reshape(group, self.features)
+            gate = jnp.dot(slab, gate_w[:, at], preferred_element_type=F32)
+            upper = jnp.dot(slab, up_w[:, at], preferred_element_type=F32)
+            self.hidden[:, at] = (gate * (1.0 / (1.0 + jnp.exp(-gate))) * upper).astype(BF16)
+            return carry
+
+        tiles = ff // width
+        lax.fori_loop(int(first * tiles), int(last * tiles), tile, 0)
+
+    def weigh(self):
+        group = self.hidden.shape[0]
+        parts = self.held[:, :, :, :, self.features :].reshape(group, LANES).astype(F32)
+        lane = lax.broadcasted_iota(jnp.int32, (group, LANES), 1)
+        experts = 4 * self.layers
+        mine = (lane % experts == self.place.ep) & (lane < 3 * experts)
+        self.scaled[...] = jnp.sum(jnp.where(mine, parts, 0.0), axis=1, keepdims=True)
+
+    def leave(self, first, last):
+        down_w = self.weights[2]
+        rows = self.held.shape[3]
+
+        def tile(i, carry):
+            at = pl.ds(pl.multiple_of(i * TILE, TILE), TILE)
+            out = jnp.dot(self.hidden[...], down_w[:, at], preferred_element_type=F32)
+            out = (out * self.scaled[...]).astype(BF16)
+            self.partial[:, :, :, :, at] = out.reshape(2, 2, self.layers, rows, TILE)
+            return carry
+
+        tiles = self.features // TILE
+        lax.fori_loop(int(first * tiles), int(last * tiles), tile, 0)
+
+    def core_sum(self, side):
+        return remote(
+            self.partial.at[side, 1 - self.place.c], self.core_in.at[side],
+            self.rs_cs.at[side], self.rs_cr.at[side], self.place.sibling,
+        )
+
+    def x_sum(self, block):
+        return remote(
+            self.x_out.at[block], self.x_in.at[block], self.rs_xs.at[block],
+            self.rs_xr.at[block], self.place.across,
+        )
+
+    def z_sum(self, way, block):
+        return remote(
+            self.z_out.at[block], self.z_in.at[way, block], self.rs_zs.at[block],
+            self.rs_zr.at[way, block], self.peers[way],
+        )
+
+    def outward(self, then, far):
+        z = self.place.z
+
+        @pl.when(z + far < self.layers)
+        def _():
+            then(0, z + far)
+
+        @pl.when(z - far >= 0)
+        def _():
+            then(1, z - far)
+
+    def sum_start(self):
+        self.core_sum(1 - self.place.x).start()
+        self.core_sum(self.place.x).start()
+
+    def sum_across(self):
+        x, c = self.place.x, self.place.c
+        self.core_sum(1 - x).wait_recv()
+
+        def send(way, block):
+            total = self.partial[1 - x, c, block].astype(F32)
+            total = total + self.core_in[1 - x, block].astype(F32)
+            self.x_out[block] = total.astype(BF16)
+            self.x_sum(block).start()
+
+        for far in range(self.layers - 1, 0, -1):
+            self.outward(send, far)
+        send(0, self.place.z)
+        self.core_sum(x).wait_recv()
+
+    def chip_total(self, block):
+        x, c = self.place.x, self.place.c
+        total = self.partial[x, c, block].astype(F32) + self.core_in[x, block].astype(F32)
+        self.x_sum(block).wait_recv()
+        return total + self.x_in[block].astype(F32)
+
+    def sum_along(self, far):
+        def send(way, block):
+            total = self.chip_total(block)
+
+            @pl.when(self.behind[way])
+            def _():
+                self.z_sum(way, block).wait_recv()
+
+            self.z_out[block] = (total + self.z_in[way, block].astype(F32)).astype(BF16)
+            self.z_sum(way, block).start()
+
+        self.outward(send, far)
+
+    def sum_end(self):
+        z = self.place.z
+        total = self.chip_total(z)
+        for way in range(2):
+            @pl.when(self.behind[way])
+            def _(way=way):
+                self.z_sum(way, z).wait_recv()
+
+            total = total + self.z_in[way, z].astype(F32)
+        return total
+
+    def finish(self):
+        x, c, z = self.place.x, self.place.c, self.place.z
+        for way in range(2):
+            @pl.when(self.ahead[way])
+            def _(way=way):
+                self.z_copy(way, 0, z).wait_send()
+
+        for step in range(self.layers - 1):
+            def sent(way, block, step=step):
+                @pl.when(self.ahead[way])
+                def _():
+                    self.z_copy(way, step + 1, block).wait_send()
+
+            self.arrivals(step, sent)
+        for block in range(self.layers):
+            self.x_copy(x, block).wait_send()
+            self.c_copy(x, c, block).wait_send()
+            self.c_copy(1 - x, c, block).wait_send()
+            self.x_sum(block).wait_send()
+        for side in range(2):
+            self.core_sum(side).wait_send()
+        for far in range(self.layers - 1, 0, -1):
+            self.outward(lambda way, block: self.z_sum(way, block).wait_send(), far)
+
+
+def run_halves(first, second, wait_weights):
+    layers = first.layers
+    first.gather_start()
+    second.gather_start()
+    for step in range(layers):
+        first.gather_step(step)
+    second.gather_step(0)
+    first.gather_end()
+    wait_weights(0)
+    first.weigh()
+    pieces = layers - 1
+    for piece in range(pieces):
+        first.enter(piece / pieces, (piece + 1) / pieces)
+        second.gather_step(piece + 1)
+    wait_weights(1)
+    first.leave(0, 1)
+    first.sum_start()
+    second.gather_end()
+    second.weigh()
+    second.enter(0, 0.34)
+    first.sum_across()
+    second.enter(0.34, 1)
+    for far in range(layers - 1, 0, -1):
+        first.sum_along(far)
+        done = layers - 1 - far
+        second.leave(done / pieces, (done + 1) / pieces)
+    second.sum_start()
+    top = first.sum_end()
+    second.sum_across()
+    for far in range(layers - 1, 0, -1):
+        second.sum_along(far)
+    return top, second.sum_end()
+
+
+def clear_ends(place, z_in):
+    for way, has in enumerate((place.has_down, place.has_up)):
+        @pl.when(jnp.logical_not(has))
+        def _(way=way):
+            z_in[way] = jnp.zeros(z_in.shape[1:], z_in.dtype)
+
+
+PHASE_REFS = 21
+
+
+def step_kernel(
+    layers,
+    rows_ref, route_ref, weight_ref, gain_ref, owner_ref, talk_route_ref, talk_weight_ref,
+    gate_hbm, up_hbm, down_hbm, proj_hbm, tgate_hbm, tup_hbm, tdown_hbm,
+    think_out, talk_out,
+    gate_v, up_v, down_v, proj_v, tgate_v, tup_v, tdown_v, load_sem,
+    *phases,
+):
+    place = Place(layers)
+    scratches = [phases[i : i + PHASE_REFS] for i in range(0, len(phases), PHASE_REFS)]
+    pairs = (
+        (gate_hbm.at[0], gate_v), (up_hbm.at[0], up_v), (down_hbm.at[0], down_v),
+        (proj_hbm, proj_v),
+        (tgate_hbm.at[0], tgate_v), (tup_hbm.at[0], tup_v), (tdown_hbm.at[0], tdown_v),
+    )
+    loads = [
+        pltpu.make_async_copy(src, dst, load_sem.at[i]) for i, (src, dst) in enumerate(pairs)
+    ]
+    experts = 4 * layers
+    rows, features = rows_ref.shape
+    half = rows // 2
+    talk_features = gain_ref.shape[1]
+    z, x, c = place.z, place.x, place.c
+    thinks = [Mixture(place, features, (gate_v, up_v, down_v), s) for s in scratches[:2]]
+    talks = [Mixture(place, talk_features, (tgate_v, tup_v, tdown_v), s) for s in scratches[2:]]
+    cuts = (pl.ds(0, half), pl.ds(half, half))
+    think_parts = dense_weights(route_ref[...], weight_ref[...], experts)
+    talk_parts = dense_weights(talk_route_ref[...], talk_weight_ref[...], experts)
+    for i, cut in enumerate(cuts):
+        own = slice(i * half, (i + 1) * half)
+        thinks[i].held[x, c, z, :, :features] = rows_ref[cut, :]
+        thinks[i].held[x, c, z, :, features:] = think_parts[own]
+        talks[i].held[x, c, z, :, talk_features:] = talk_parts[own]
+        clear_ends(place, thinks[i].z_in)
+        clear_ends(place, talks[i].z_in)
+    greet(place)
+    for load in loads:
+        load.start()
+
+    def wait_think(stage):
+        for load in (loads[:2], loads[2:3])[stage]:
+            load.wait()
+
+    def wait_talk(stage):
+        for load in (loads[4:6], loads[6:7])[stage]:
+            load.wait()
+
+    totals = run_halves(*thinks, wait_think)
+    branch = jnp.concatenate(totals, axis=0).astype(BF16)
+    think_out[...] = branch
+    loads[3].wait()
+    projected = jnp.dot(branch, proj_v[...], preferred_element_type=F32).astype(BF16)
+    count = owner_ref.shape[1]
+    spot = lax.broadcasted_iota(jnp.int32, (count, count), 0)
+    picker = jnp.where(owner_ref[...] == spot, 1.0, 0.0).astype(BF16)
+    own_rows = lax.dot_general(
+        picker, projected, (((0,), (0,)), ((), ())), preferred_element_type=F32
+    )
+    scale = lax.rsqrt(jnp.mean(own_rows * own_rows, axis=1, keepdims=True) + 1e-06)
+    talk_rows = (own_rows * scale * gain_ref[...]).astype(BF16)
+    for i in range(2):
+        talks[i].held[x, c, z, :, :talk_features] = talk_rows[i * half : (i + 1) * half]
+    totals = run_halves(*talks, wait_talk)
+    talk_out[...] = jnp.concatenate(totals, axis=0).astype(BF16)
+    for mixture in thinks + talks:
+        mixture.finish()
+
+
+def hand_over(think_in, talk_in, think_out, talk_out, sem):
+    copies = [
+        pltpu.make_async_copy(src, dst, sem.at[i])
+        for i, (src, dst) in enumerate(((think_in, think_out), (talk_in, talk_out)))
+    ]
+    for copy in copies:
+        copy.start()
+    for copy in copies:
+        copy.wait()
+
+
+def phase_scratch(layers, rows, features, ff):
+    group = 4 * layers * rows
+    dma = pltpu.SemaphoreType.DMA
+    block = (layers, rows, features)
+    return [
+        pltpu.VMEM((2, 2, layers, rows, features + LANES), BF16),
+        pltpu.VMEM((group, ff), BF16),
+        pltpu.VMEM((group, 1), F32),
+        pltpu.VMEM((2, 2) + block, BF16),
+        pltpu.VMEM((2,) + block, BF16),
+        pltpu.VMEM(block, BF16),
+        pltpu.VMEM(block, BF16),
+        pltpu.VMEM(block, BF16),
+        pltpu.VMEM((2,) + block, BF16),
+        dma((2, layers)), dma((2, layers)),
+        dma((layers,)), dma((layers,)),
+        dma((2, layers)), dma((2, layers)),
+        dma((2,)), dma((2,)),
+        dma((layers,)), dma((layers,)),
+        dma((layers,)), dma((2, layers)),
+    ]
+
+
+def dense_on_device(
+    thinker_rows, think_route, think_weight, think_gate, think_up, think_down, proj_weight,
+    owner_map, talk_gain, talk_route, talk_weight, talk_gate, talk_up, talk_down,
+):
+    layers = lax.axis_size("ep") // 4
+    rows, features = thinker_rows.shape
+    talk_features, talk_ff = talk_gate.shape[1:]
+    ff = think_gate.shape[2]
+    vmem = pl.BlockSpec(memory_space=pltpu.VMEM)
+    hbm = pl.BlockSpec(memory_space=pl.ANY)
+    weights = (think_gate, think_up, think_down, proj_weight, talk_gate, talk_up, talk_down)
+    sizes = [w.shape[-2:] for w in weights]
+    all_rows = 4 * layers * rows
+    outs = (
+        jax.ShapeDtypeStruct((rows, features), BF16),
+        jax.ShapeDtypeStruct((rows, talk_features), BF16),
+    )
+    branches = pl.pallas_call(
+        functools.partial(step_kernel, layers),
+        out_shape=outs,
+        in_specs=[vmem] * 7 + [hbm] * 7,
+        out_specs=(vmem, vmem),
+        scratch_shapes=[pltpu.VMEM(size, BF16) for size in sizes]
+        + [pltpu.SemaphoreType.DMA((len(sizes),))]
+        + 2 * phase_scratch(layers, rows // 2, features, ff)
+        + 2 * phase_scratch(layers, rows // 2, talk_features, talk_ff),
+        compiler_params=pltpu.CompilerParams(
+            collective_id=0, has_side_effects=True, vmem_limit_bytes=56 * 1024 * 1024
+        ),
+        cost_estimate=pl.CostEstimate(
+            flops=6 * all_rows * (features * ff + talk_features * talk_ff),
+            bytes_accessed=2 * sum(a * b for a, b in sizes),
+            transcendentals=all_rows * (ff + talk_ff),
+        ),
+    )(
+        thinker_rows, think_route.T, think_weight.T, talk_gain[None, :], owner_map[None, :],
+        talk_route.T, talk_weight.T, *weights,
+    )
+    return pl.pallas_call(
+        hand_over,
+        out_shape=outs,
+        in_specs=[hbm, hbm],
+        out_specs=(hbm, hbm),
+        scratch_shapes=[pltpu.SemaphoreType.DMA((2,))],
+    )(*branches)
+
+
+def on_device(*arguments):
+    rows, picks = arguments[1].shape
+    ep_count = lax.axis_size("ep")
+    whole = lax.axis_size("sess") == 1 and ep_count % 4 == 0 and 3 * ep_count <= LANES
+    whole = whole and ep_count >= 8 and rows % 32 == 0 and 2 * picks >= ep_count
+    if whole and arguments[0].shape[1] % TILE == 0 and arguments[8].shape[0] % TILE == 0:
+        return dense_on_device(*arguments)
+    return packed_on_device(*arguments)
+
+
 def solution(mesh):
     return jax.shard_map(
         on_device,

time: 200 us -> 114 us (0.57)
  Pallas kernels: 0 us -> 113 us
  blocking collectives: 86.4 us -> 0 us
  waiting for transfers between devices: 57.6 us -> 0 us
  local copies, waits for them, and re-layouts: 20.7 us -> 0 us
  matrix products: 16.4 us -> 0 us
  starting transfers between devices: 9.58 us -> 0 us
  other arithmetic: 7.37 us -> 0 us
    pallas_call x0 -> x2, Pallas kernels: none -> 113 us  [the longest x1 106 us: dense_on_device(): pl.pallas_call(functools.partial(step_kernel, layers), out_shape=outs, in...]
    all_to_all x2 -> x0, blocking collectives: 86.4 us -> none  [the longest x1 54.9 us: on_device(): lax.all_to_all(paired, 'ep', split_axis=0, concat_axis=0, tiled=True)]
    all_to_all x2 -> x0, waiting for transfers between devices: 57.6 us -> none  [the longest x1 39.6 us: on_device(): lax.all_to_all(summed, 'ep', split_axis=0, concat_axis=0, tiled=True)]
    dot_general x6 -> x0, matrix products: 16.4 us -> none  [the longest x2 6.85 us: swiglu(): return jnp.dot(hidden, down_m, preferred_element_type=jnp.float32)]
    all_to_all x2 -> x0, starting transfers between devices: 9.58 us -> none  [the longest x1 5.3 us: on_device(): lax.all_to_all(summed, 'ep', split_axis=0, concat_axis=0, tiled=True)]
    gather x2 -> x0, local copies, waits for them, and re-layouts: 7.89 us -> none  [combine_rows(): returned[target].astype(jnp.float32)]
    scatter x2 -> x0, local copies, waits for them, and re-layouts: 6.46 us -> none  [pack_rows(): jnp.zeros((experts * capacity, row_block.shape[1]), jnp.bfloat16).at[target]]
    reduce_sum x6 -> x0, other arithmetic: 4.62 us -> none  [the longest x2 4.46 us: combine_rows(): jnp.sum(gathered * norm_weights[:, :, None], axis=1).astype(jnp.bfloat16)]
  transfers between devices with their start and end apart: 2 -> 0, of which waited for: 2 -> 0; matrix products, arithmetic and copies ran while one was open for 1% -> 0% of each run, Pallas kernels for 0% -> 0%
where the time goes in v2:
time: 114 us
  Pallas kernels  113 us (99%)
    pallas_call x1, Pallas kernels, dense_on_device(): pl.pallas_call(functools.partial(step_kernel, layers), out_shape=outs, in...  106 us
    pallas_call x1, Pallas kernels, dense_on_device(): pl.pallas_call(hand_over, out_shape=outs, in_specs=[hbm, hbm], out_specs=...  7.08 us

profile of v2, /device:TPU:0, one launch (start us, length us, event | category | flops | bytes accessed | tf_op | source)
XLA Modules:
  0.0 114.1 jit_solution(6216655811784490667)
XLA Ops:
  0.6 106.4 %shard_map.149 = (bf16[32,2048]{1,0:T(8,128)(2,1)}, bf16[32,1024]{1,0:T(8,128)(2,1)}) custom-call(bf16[32,2048]{1,0:T(8,128)(2,1)} %rows_ref.1, s32[8,32]{1,0:T(8,128)} %bitcast.6, f32[8,32]{1,0:T(8,128)} %bitcast.7, f32[1,1024]{1,0:T(1,128)} %bitcast.8, s32[1,32]{1,0:T(1,128)} %bitcast.11, s32[6,32]{1,0:T(8,128)} %bitcast.9, f32[6,32]{1,0:T(8,128)} %bitcast.10, ...), custom_call_target="tpu_custom_call" | custom-call | flops 6039797760 | bytes 15990784 | tf_op jit(solution)/shard_map/pallas_call | solution.py:575
  107.0 7.1 %shard_map.150 = (bf16[32,2048]{1,0:T(8,128)(2,1)}, bf16[32,1024]{1,0:T(8,128)(2,1)}) custom-call(bf16[32,2048]{1,0:T(8,128)(2,1)} %get-tuple-element.4.think_in, bf16[32,1024]{1,0:T(8,128)(2,1)} %get-tuple-element.5.talk_in), custom_call_target="tpu_custom_call" | custom-call | tf_op jit(solution)/shard_map/pallas_call | solution.py:596

commit v3 on v1

--- a/solution.py
+++ b/solution.py
@@ -121,20 +121,26 @@
 
 
 def dense_weights(route, weights, experts):
-    rows, picks = route.shape
-    lane = lax.broadcasted_iota(jnp.int32, (rows, LANES), 1)
-    norm = weights / jnp.sum(weights, axis=1, keepdims=True)
-    parts = jnp.zeros((rows, LANES), F32)
+    picks, rows = route.shape
+    spot = lax.broadcasted_iota(jnp.int32, (LANES, rows), 0)
+    norm = weights / jnp.sum(weights, axis=0, keepdims=True)
+    parts = jnp.zeros((LANES, rows), F32)
     for k in range(picks):
-        value = norm[:, k : k + 1]
+        value = norm[k : k + 1]
         high = value.astype(BF16).astype(F32)
         middle = (value - high).astype(BF16).astype(F32)
         low = value - high - middle
-        chosen = route[:, k : k + 1]
-        parts = parts + jnp.where(lane == chosen, high, 0.0)
-        parts = parts + jnp.where(lane == chosen + experts, middle, 0.0)
-        parts = parts + jnp.where(lane == chosen + 2 * experts, low, 0.0)
-    return parts.astype(BF16)
+        chosen = route[k : k + 1]
+        parts = parts + jnp.where(spot == chosen, high, 0.0)
+        parts = parts + jnp.where(spot == chosen + experts, middle, 0.0)
+        parts = parts + jnp.where(spot == chosen + 2 * experts, low, 0.0)
+    down = lax.broadcasted_iota(jnp.int32, (rows, rows), 0)
+    along = lax.broadcasted_iota(jnp.int32, (rows, rows), 1)
+    turned = lax.dot_general(
+        jnp.where(down == along, 1.0, 0.0).astype(BF16), parts.astype(BF16),
+        (((1,), (1,)), ((), ())), preferred_element_type=F32,
+    )
+    return turned.astype(BF16)
 
 
 class Place:
@@ -433,10 +439,12 @@
     think_out[...] = branch
     loads[3].wait()
     projected = jnp.dot(branch, proj_v[...], preferred_element_type=F32).astype(BF16)
-    count = owner_ref.shape[0]
-    spot = lax.broadcasted_iota(jnp.int32, (count, count), 1)
+    count = owner_ref.shape[1]
+    spot = lax.broadcasted_iota(jnp.int32, (count, count), 0)
     picker = jnp.where(owner_ref[...] == spot, 1.0, 0.0).astype(BF16)
-    own_rows = jnp.dot(picker, projected, preferred_element_type=F32)
+    own_rows = lax.dot_general(
+        picker, projected, (((0,), (0,)), ((), ())), preferred_element_type=F32
+    )
     scale = lax.rsqrt(jnp.mean(own_rows * own_rows, axis=1, keepdims=True) + 1e-06)
     talk_held[x, c, z, :, :talk_features] = (own_rows * scale * gain_ref[...]).astype(BF16)
     total, finish_talk = mixture_phase(
@@ -445,6 +453,17 @@
     talk_out[...] = total.astype(BF16)
     finish_think()
     finish_talk()
+
+
+def hand_over(think_in, talk_in, think_out, talk_out, sem):
+    copies = [
+        pltpu.make_async_copy(src, dst, sem.at[i])
+        for i, (src, dst) in enumerate(((think_in, think_out), (talk_in, talk_out)))
+    ]
+    for copy in copies:
+        copy.start()
+    for copy in copies:
+        copy.wait()
 
 
 def phase_scratch(layers, rows, features, ff):
@@ -483,12 +502,13 @@
     weights = (think_gate, think_up, think_down, proj_weight, talk_gate, talk_up, talk_down)
     sizes = [w.shape[-2:] for w in weights]
     all_rows = 4 * layers * rows
-    return pl.pallas_call(
+    outs = (
+        jax.ShapeDtypeStruct((rows, features), BF16),
+        jax.ShapeDtypeStruct((rows, talk_features), BF16),
+    )
+    branches = pl.pallas_call(
         functools.partial(step_kernel, layers),
-        out_shape=(
-            jax.ShapeDtypeStruct((rows, features), BF16),
-            jax.ShapeDtypeStruct((rows, talk_features), BF16),
-        ),
+        out_shape=outs,
         in_specs=[vmem] * 7 + [hbm] * 7,
         out_specs=(vmem, vmem),
         scratch_shapes=[pltpu.VMEM(size, BF16) for size in sizes]
@@ -504,9 +524,16 @@
             transcendentals=all_rows * (ff + talk_ff),
         ),
     )(
-        thinker_rows, think_route, think_weight, talk_gain[None, :], owner_map[:, None],
-        talk_route, talk_weight, *weights,
-    )
+        thinker_rows, think_route.T, think_weight.T, talk_gain[None, :], owner_map[None, :],
+        talk_route.T, talk_weight.T, *weights,
+    )
+    return pl.pallas_call(
+        hand_over,
+        out_shape=outs,
+        in_specs=[hbm, hbm],
+        out_specs=(hbm, hbm),
+        scratch_shapes=[pltpu.SemaphoreType.DMA((2,))],
+    )(*branches)
 
 
 def on_device(*arguments):

time: 94.4 us -> 91 us (0.964)
  local copies, waits for them, and re-layouts: 9.84 us -> 0 us
  Pallas kernels: 83.6 us -> 90.2 us
    unnamed x6 -> x0, local copies, waits for them, and re-layouts: 8.51 us -> none
    pallas_call x1 -> x2, Pallas kernels: 83.6 us -> 90.2 us  [the longest x1 83.1 us: dense_on_device(): pl.pallas_call(functools.partial(step_kernel, layers), out_shape=outs, in...]
    broadcast_in_dim x1 -> x0, local copies, waits for them, and re-layouts: 1.33 us -> none  [dense_on_device(): owner_map[:, None]]
where the time goes in v3:
time: 91 us; the launch traced here: 90.8 us
  Pallas kernels  90.2 us (99%)
    pallas_call x1, Pallas kernels, dense_on_device(): pl.pallas_call(functools.partial(step_kernel, layers), out_shape=outs, in...  83.1 us
    pallas_call x1, Pallas kernels, dense_on_device(): pl.pallas_call(hand_over, out_shape=outs, in_specs=[hbm, hbm], out_specs=...  7.08 us

profile of v3, /device:TPU:0, one launch (start us, length us, event | category | flops | bytes accessed | tf_op | source)
XLA Modules:
  0.0 90.8 jit_solution(4308519490226886232)
XLA Ops:
  0.6 83.1 %shard_map.149 = (bf16[32,2048]{1,0:T(8,128)(2,1)}, bf16[32,1024]{1,0:T(8,128)(2,1)}) custom-call(bf16[32,2048]{1,0:T(8,128)(2,1)} %rows_ref.1, s32[8,32]{1,0:T(8,128)} %bitcast.6, f32[8,32]{1,0:T(8,128)} %bitcast.7, f32[1,1024]{1,0:T(1,128)} %bitcast.8, s32[1,32]{1,0:T(1,128)} %bitcast.11, s32[6,32]{1,0:T(8,128)} %bitcast.9, f32[6,32]{1,0:T(8,128)} %bitcast.10, ...), custom_call_target="tpu_custom_call" | custom-call | flops 6039797760 | bytes 15990784 | tf_op jit(solution)/shard_map/pallas_call | solution.py:509
  83.7 7.1 %shard_map.150 = (bf16[32,2048]{1,0:T(8,128)(2,1)}, bf16[32,1024]{1,0:T(8,128)(2,1)}) custom-call(bf16[32,2048]{1,0:T(8,128)(2,1)} %get-tuple-element.4.think_in, bf16[32,1024]{1,0:T(8,128)(2,1)} %get-tuple-element.5.talk_in), custom_call_target="tpu_custom_call" | custom-call | tf_op jit(solution)/shard_map/pallas_call | solution.py:530
